TPU v7x, 32 devices: a whole 2x2x4 slice. The times are simulated.
32 devices in a mesh: leaf: 16 (over z, y, x), front: 2 (over core).
Axes of the slice: x: 2, y: 2, z: 4, core: 2. Of those that a mesh axis runs over, the one named last changes fastest.
Arguments:
- child_pivot: float32 [32, 1152, 1152], P('leaf', 'front'), as said below
- child_lower: float32 [32, 192, 1152], P('leaf', 'front'), as said below
- child_tail: float32 [32, 192, 192], P('leaf', 'front'), as said below
- child_map: int32 [32, 192], replicated, may hold values from 0 to 1151, as said below
- child_parent: int32 [32, 1], replicated, may hold values from 0 to 15, as said below
- owner: int32 [16], replicated, may hold values from 0 to 15, as said below
- parent_front: float32 [16, 1152, 1152], P('leaf', 'front'), as said below
Outputs:
- child_diag: float32 [32, 1152, 1152], P('leaf', 'front')
- child_below: float32 [32, 192, 1152], P('leaf', 'front')
- parent_factor: float32 [16, 1152, 1152], P('leaf', 'front')
Inputs may be any that keep to these rules, and one draw needn't show every extreme that they name: For each child c the symmetric matrix with blocks child_pivot[c], child_lower[c]^T in the upper right, child_lower[c] and child_tail[c] is positive definite, with camera blocks of 6 rows and columns. `child_lower`: same matrices as stated for child_pivot. `child_tail`: same matrices as stated for child_pivot. Each parent_front[g] is symmetric positive definite. `child_map`: within one child the entries are distinct; entries k * 192 // 2 to (k + 1) * 192 // 2 - 1 lie in k * 1152 // 2 to (k + 1) * 1152 // 2 - 1, for k below 2. `child_parent`: every parent has at least one child. Child 2 * g, the first child of leaf group g, has a parent owned by group (g + 8) mod 16; the other children's parents are spread unevenly. `owner`: each leaf group owns exactly one parent.
All inputs are finite; a program needn't handle non-finite values.
Results may differ from a plain program's by a relative error of at most 0.00005.
Values sent between devices are 32-bit elements; how exact they have to be, the bound alone decides.
A program may use at most 192 MiB of HBM per device.

v0:
```python
import functools
import itertools

import jax
import jax.numpy as jnp
from jax import lax
from jax.experimental import pallas as pl
from jax.experimental.pallas import tpu as pltpu
from jax.sharding import PartitionSpec as P

NB = 128
PW = 16
F32 = jnp.float32
BF16 = jnp.bfloat16


def split(x):
    high = x.astype(BF16)
    low = (x - high.astype(F32)).astype(BF16)
    return high, low


def rows_dot(a, b):
    return lax.dot_general(a, b, (((1,), (1,)), ((), ())), preferred_element_type=F32)


def cols_dot(a, b):
    return lax.dot_general(a, b, (((0,), (0,)), ((), ())), preferred_element_type=F32)


def factor_block(work):
    row = lax.broadcasted_iota(jnp.int32, (PW, NB), 0)
    for panel in range(NB // PW):
        first = panel * PW
        left = work[first : first + PW, :NB]
        right = work[first : first + PW, NB:]
        cols = [
            jnp.broadcast_to(left[:, first + j : first + j + 1], (PW, NB)) for j in range(PW)
        ]
        for j in range(PW):
            inv = lax.rsqrt(jnp.broadcast_to(cols[j][j : j + 1], (PW, NB)))
            scaled = jnp.where(row > j, cols[j] * inv, 0.0)
            left_row = jnp.broadcast_to(left[j : j + 1], (PW, NB)) * inv
            right_row = jnp.broadcast_to(right[j : j + 1], (PW, NB)) * inv
            left = jnp.where(row == j, left_row, left - scaled * left_row)
            right = jnp.where(row == j, right_row, right - scaled * right_row)
            for k in range(j + 1, PW):
                cols[k] = cols[k] - scaled * (
                    jnp.broadcast_to(cols[k][j : j + 1], (PW, NB)) * inv
                )
        work[first : first + PW, :NB] = left
        work[first : first + PW, NB:] = right
        if first + PW < NB:
            left_high, left_low = split(left)
            right_high, right_low = split(right)
            both_high = jnp.concatenate([left_high, right_high], axis=1)
            both_low = jnp.concatenate([left_low, right_low], axis=1)
            update = cols_dot(
                jnp.concatenate([left_high, left_high, left_low], axis=0),
                jnp.concatenate([both_high, both_low, both_high], axis=0),
            )
            work[first + PW :, :] = work[first + PW :, :] - update[first + PW :, :]


def factor_front(front, panel, work, pivots, rows):
    blocks = pivots // NB
    row = lax.broadcasted_iota(jnp.int32, (NB, NB), 0)
    col = lax.broadcasted_iota(jnp.int32, (NB, NB), 1)

    def step(block, carry):
        base = pl.multiple_of(block * NB, NB)
        work[:, :NB] = front[pl.ds(base, NB), pl.ds(base, NB)]
        work[:, NB:] = jnp.where(row == col, 1.0, 0.0)
        factor_block(work)
        front[pl.ds(base, NB), pl.ds(base, NB)] = jnp.where(
            row >= col, jnp.transpose(work[:, :NB]), 0.0
        )
        inv_high, inv_low = split(work[:, NB:])
        inv_twice = jnp.concatenate([inv_high, inv_high], axis=1)
        for at in range(blocks):

            @pl.when(block == at)
            def _():
                here = at * NB
                after = here + NB
                if at:
                    front[:here, here:after] = jnp.zeros((here, NB), F32)
                if after >= rows:
                    return
                high, low = split(front[after:rows, here:after])
                solved = rows_dot(jnp.concatenate([high, low], axis=1), inv_twice)
                solved = solved + rows_dot(high, inv_low)
                front[after:rows, here:after] = solved
                high, low = split(solved)
                panel[after:rows, :NB] = high
                panel[after:rows, NB:] = low

                def tile(index, carry):
                    start = pl.multiple_of(after + index * 2 * NB, NB)
                    col_high = panel[pl.ds(start, 2 * NB), :NB]
                    col_low = panel[pl.ds(start, 2 * NB), NB:]
                    update = rows_dot(
                        panel[after:rows, :], jnp.concatenate([col_high, col_high], axis=1)
                    )
                    update = update + rows_dot(panel[after:rows, :NB], col_low)
                    front[after:rows, pl.ds(start, 2 * NB)] = (
                        front[after:rows, pl.ds(start, 2 * NB)] - update
                    )
                    return carry

                lax.fori_loop(0, -(-(rows - after) // (2 * NB)), tile, 0)

        return carry

    lax.fori_loop(0, blocks, step, 0)


def padded(rows):
    return -(-rows // NB) * NB + NB


def pack(front, packed, start, contrib):
    third = contrib // 3
    a, b, c, end = start, start + third, start + 2 * third, start + contrib
    packed[:third, :] = jnp.concatenate([front[a:b, a:b], front[b:c, b:c]], axis=1)
    packed[third : 2 * third, :] = front[c:end, a:c]
    packed[2 * third :, :] = jnp.concatenate([front[b:c, a:b], front[c:end, c:end]], axis=1)


def unpack(packed):
    third = packed.shape[0] // 3
    diag, last, mixed = packed[:third], packed[third : 2 * third], packed[2 * third :]
    last_t = jnp.transpose(last)
    mixed_t = jnp.transpose(mixed)
    top = jnp.concatenate([diag[:, :third], mixed_t[:third], last_t[:third]], axis=1)
    middle = jnp.concatenate([mixed[:, :third], diag[:, third:], last_t[third:]], axis=1)
    bottom = jnp.concatenate([last, mixed_t[third:]], axis=1)
    return jnp.concatenate([top, middle, bottom], axis=0)


def exchange_kernel(
    groups, packed, first, others, swap, held, swap_sems, first_sems, send_sems, recv_sems,
    front_send, front_recv,
):
    member = lax.axis_index("front")
    group = lax.axis_index("leaf")
    half = packed.shape[0] // 2
    mine = pl.multiple_of(member * half, 8)
    theirs = pl.multiple_of((1 - member) * half, 8)
    rows = pl.ds(mine, half)
    strides = []
    stride = groups
    while stride > 1:
        stride = stride // 4
        strides.append(stride)
    digits = [(group // stride) % 4 for stride in strides]

    def at(shifts):
        return sum(
            ((digit + shift) % 4) * stride
            for digit, shift, stride in zip(digits, shifts, strides)
        )

    def unit(stage, shift):
        return tuple(shift if s == stage else 0 for s in range(len(strides)))

    other_core = {"front": 1 - member}
    mesh = pl.DeviceIdType.MESH
    barrier = pltpu.get_barrier_semaphore()
    pl.semaphore_signal(barrier, inc=1, device_id=other_core, device_id_type=mesh)
    for stage in range(len(strides)):
        for shift in range(1, 4):
            pl.semaphore_signal(
                barrier, inc=1, device_id={"leaf": at(unit(stage, shift))}, device_id_type=mesh
            )
    pl.semaphore_wait(barrier, 1 + 3 * len(strides))

    def remote(src, dst, send_sem, recv_sem, device):
        return pltpu.make_async_remote_copy(
            src_ref=src,
            dst_ref=dst,
            send_sem=send_sem,
            recv_sem=recv_sem,
            device_id=device,
            device_id_type=mesh,
        )

    started = []
    swapped = remote(
        packed.at[pl.ds(theirs, half)], swap, swap_sems.at[0], swap_sems.at[1], other_core
    )
    swapped.start()
    swapped.wait()
    own = packed[rows, :]
    got = swap[...]
    held[...] = jnp.where(member == 0, own, got)
    others[group, rows, :] = jnp.where(member == 0, got, own)

    sent = 0
    arrivals = {}
    order = sorted(
        itertools.product(range(4), repeat=len(strides)),
        key=lambda shifts: max([s for s in range(len(strides)) if shifts[s]], default=-1),
    )
    first_copy = None
    for shifts in order:
        block = at(shifts)
        stage = max([s for s in range(len(strides)) if shifts[s]], default=-1)
        here = others.at[block, rows]
        if stage >= 0:
            remote(here, here, send_sems.at[0], recv_sems.at[block], other_core).wait_recv()
        for later in range(stage + 1, len(strides)):
            for shift in (2, 1, 3):
                copy = remote(
                    here, here, send_sems.at[sent], recv_sems.at[block],
                    {"leaf": at(unit(later, shift))},
                )
                copy.start()
                started.append(copy)
                sent += 1
            if stage < 0 and later == 0:
                first_copy = remote(
                    held, first.at[rows], first_sems.at[0], first_sems.at[1],
                    {"leaf": at(unit(0, 2))},
                )
                first_copy.start()
        across = remote(here, here, front_send.at[block], front_recv.at[block], other_core)
        across.start()
        arrivals[shifts] = across
    first_copy.wait_recv()
    first_across = remote(
        first.at[rows], first.at[rows], first_sems.at[2], first_sems.at[3], other_core
    )
    first_across.start()
    first_copy.wait_send()
    for copy in started:
        copy.wait_send()
    theirs_rows = pl.ds(theirs, half)
    for shifts, across in arrivals.items():
        block = at(shifts)
        across.wait_send()
        there = others.at[block, theirs_rows]
        remote(there, there, front_send.at[block], front_recv.at[block], other_core).wait_recv()
    first_across.wait_send()
    there = first.at[theirs_rows]
    remote(there, there, first_sems.at[2], first_sems.at[3], other_core).wait_recv()


def exchange(packed, groups):
    rows, cols = packed.shape
    vmem = pl.BlockSpec(memory_space=pltpu.VMEM)
    return pl.pallas_call(
        functools.partial(exchange_kernel, groups),
        out_shape=(
            jax.ShapeDtypeStruct((rows, cols), F32),
            jax.ShapeDtypeStruct((groups, rows, cols), F32),
        ),
        in_specs=[vmem],
        out_specs=(vmem, vmem),
        scratch_shapes=[
            pltpu.VMEM((rows // 2, cols), F32),
            pltpu.VMEM((rows // 2, cols), F32),
            pltpu.SemaphoreType.DMA((2,)),
            pltpu.SemaphoreType.DMA((4,)),
            pltpu.SemaphoreType.DMA((groups,)),
            pltpu.SemaphoreType.DMA((groups,)),
            pltpu.SemaphoreType.DMA((groups,)),
            pltpu.SemaphoreType.DMA((groups,)),
        ],
        compiler_params=pltpu.CompilerParams(
            collective_id=0, has_side_effects=True, vmem_limit_bytes=40 * 2**20
        ),
    )(packed)


def child_kernel(
    own_p, got_p, own_l, got_l, own_t, got_t, diag, diag_send, below, below_send, schur,
    front, panel, work, tail, sems,
):
    member = lax.axis_index("front")
    half = own_p.shape[1]
    pivots = half * 2
    half_c = own_l.shape[1]
    contrib = half_c * 2
    rows = pivots + contrib
    mine = pl.multiple_of(member * half, 8)
    theirs = pl.multiple_of((1 - member) * half, 8)
    mine_c = pl.multiple_of(member * half_c, 8)
    theirs_c = pl.multiple_of((1 - member) * half_c, 8)
    pivot_cols = pl.ds(0, pivots)
    copies = [
        pltpu.make_async_copy(own_p.at[member], front.at[pl.ds(mine, half), pivot_cols], sems.at[0]),
        pltpu.make_async_copy(got_p, front.at[pl.ds(theirs, half), pivot_cols], sems.at[1]),
        pltpu.make_async_copy(
            own_l.at[member], front.at[pl.ds(pivots + mine_c, half_c), pivot_cols], sems.at[2]
        ),
        pltpu.make_async_copy(
            got_l, front.at[pl.ds(pivots + theirs_c, half_c), pivot_cols], sems.at[3]
        ),
        pltpu.make_async_copy(own_t.at[member], tail.at[pl.ds(mine_c, half_c)], sems.at[4]),
        pltpu.make_async_copy(got_t, tail.at[pl.ds(theirs_c, half_c)], sems.at[5]),
    ]
    for copy in copies:
        copy.start()
    for copy in copies:
        copy.wait()
    front[pivots:rows, pivots:rows] = tail[...]
    factor_front(front, panel, work, pivots, rows)
    pack(front, schur, pivots, contrib)
    copies = [
        pltpu.make_async_copy(front.at[pl.ds(mine, half), pivot_cols], diag.at[member], sems.at[0]),
        pltpu.make_async_copy(front.at[pl.ds(theirs, half), pivot_cols], diag_send, sems.at[1]),
        pltpu.make_async_copy(
            front.at[pl.ds(pivots + mine_c, half_c), pivot_cols], below.at[member], sems.at[2]
        ),
        pltpu.make_async_copy(
            front.at[pl.ds(pivots + theirs_c, half_c), pivot_cols], below_send, sems.at[3]
        ),
    ]
    for copy in copies:
        copy.start()
    for copy in copies:
        copy.wait()


def eliminate_child(own_p, got_p, own_l, got_l, own_t, got_t):
    half, pivots = got_p.shape
    half_c, contrib = got_t.shape
    rows = pivots + contrib
    anywhere = pl.BlockSpec(memory_space=pl.ANY)
    return pl.pallas_call(
        child_kernel,
        out_shape=(
            jax.ShapeDtypeStruct(own_p.shape, F32),
            jax.ShapeDtypeStruct(got_p.shape, F32),
            jax.ShapeDtypeStruct(own_l.shape, F32),
            jax.ShapeDtypeStruct(got_l.shape, F32),
            jax.ShapeDtypeStruct((contrib, 2 * (contrib // 3)), F32),
        ),
        in_specs=[anywhere] * 6,
        out_specs=(anywhere,) * 4 + (pl.BlockSpec(memory_space=pltpu.VMEM),),
        scratch_shapes=[
            pltpu.VMEM((rows, padded(rows)), F32),
            pltpu.VMEM((padded(rows), 2 * NB), BF16),
            pltpu.VMEM((NB, 2 * NB), F32),
            pltpu.VMEM((contrib, contrib), F32),
            pltpu.SemaphoreType.DMA((6,)),
        ],
        compiler_params=pltpu.CompilerParams(vmem_limit_bytes=48 * 2**20),
    )(own_p, got_p, own_l, got_l, own_t, got_t)


def parent_kernel(
    count, picked, first, maps, own, got, first_schur, others, out,
    front, panel, work, block, sems,
):
    member = lax.axis_index("front")
    half, pivots = got.shape
    contrib = first_schur.shape[0]
    mine = pl.multiple_of(member * half, 8)
    theirs = pl.multiple_of((1 - member) * half, 8)
    pivot_cols = pl.ds(0, pivots)
    copies = [
        pltpu.make_async_copy(own.at[0], front.at[pl.ds(mine, half), pivot_cols], sems.at[0]),
        pltpu.make_async_copy(got, front.at[pl.ds(theirs, half), pivot_cols], sems.at[1]),
    ]
    for copy in copies:
        copy.start()
    for copy in copies:
        copy.wait()
    slot = lax.broadcasted_iota(jnp.int32, (pivots, contrib), 0)
    strip = 3 * NB

    def place(child, values):
        places = jnp.where(slot == maps[pl.ds(child, 1), :], 1.0, 0.0).astype(BF16)
        high, low = split(values)
        spread_high = rows_dot(high, places).astype(BF16)
        spread_low = rows_dot(low, places).astype(BF16)
        for row in range(0, pivots, strip):
            for col in range(0, row + strip, strip):
                chosen = places[row : row + strip]
                front[row : row + strip, col : col + strip] = (
                    front[row : row + strip, col : col + strip]
                    + jnp.dot(
                        chosen, spread_high[:, col : col + strip], preferred_element_type=F32
                    )
                    + jnp.dot(chosen, spread_low[:, col : col + strip], preferred_element_type=F32)
                )

    block[...] = first_schur[...]

    def add(position, carry):
        @pl.when(position > 0)
        def _():
            source = picked[jnp.maximum(position - 1, 0)]
            copy = pltpu.make_async_copy(others.at[source], block, sems.at[0])
            copy.start()
            copy.wait()

        child = jnp.where(
            position > 0, picked[jnp.maximum(position - 1, 0)] * 2 + 1, first[0] * 2
        )
        place(child, unpack(block[...]))
        return carry

    lax.fori_loop(0, count[0] + 1, add, 0)
    factor_front(front, panel, work, pivots, pivots)
    copy = pltpu.make_async_copy(front.at[pl.ds(mine, half), pivot_cols], out.at[0], sems.at[0])
    copy.start()
    copy.wait()


def eliminate_parent(count, picked, first, maps, own, got, first_schur, others):
    half, pivots = got.shape
    anywhere = pl.BlockSpec(memory_space=pl.ANY)
    scalars = pl.BlockSpec(memory_space=pltpu.SMEM)
    vmem = pl.BlockSpec(memory_space=pltpu.VMEM)
    return pl.pallas_call(
        parent_kernel,
        out_shape=jax.ShapeDtypeStruct(own.shape, F32),
        in_specs=[scalars] * 3 + [vmem, anywhere, anywhere, vmem, anywhere],
        out_specs=anywhere,
        scratch_shapes=[
            pltpu.VMEM((pivots, padded(pivots)), F32),
            pltpu.VMEM((padded(pivots), 2 * NB), BF16),
            pltpu.VMEM((NB, 2 * NB), F32),
            pltpu.VMEM(first_schur.shape, F32),
            pltpu.SemaphoreType.DMA((2,)),
        ],
        compiler_params=pltpu.CompilerParams(vmem_limit_bytes=48 * 2**20),
    )(count, picked, first, maps, own, got, first_schur, others)


def on_device(child_pivot, child_lower, child_tail, child_map, child_parent, owner, parent_front):
    member = lax.axis_index("front")
    group = lax.axis_index("leaf")
    groups = lax.axis_size("leaf")
    swap = [(0, 1), (1, 0)]

    def theirs(array):
        return lax.dynamic_index_in_dim(array, 1 - member, 0, keepdims=False)

    got_pivot = lax.ppermute(theirs(child_pivot), "front", swap)
    got_lower = lax.ppermute(theirs(child_lower), "front", swap)
    got_tail = lax.ppermute(theirs(child_tail), "front", swap)
    got_parent = lax.ppermute(parent_front[0], "front", swap)
    diag, diag_send, below, below_send, schur = eliminate_child(
        child_pivot, got_pivot, child_lower, got_lower, child_tail, got_tail
    )
    first_schur, others = exchange(schur, groups)
    diag_got = lax.ppermute(diag_send, "front", swap)
    below_got = lax.ppermute(below_send, "front", swap)

    mine = owner[child_parent[1::2, 0]] == group
    positions = jnp.arange(groups, dtype=jnp.int32)
    earlier = positions[None, :] < positions[:, None]
    rank = jnp.sum((earlier & mine[None, :]).astype(jnp.int32), axis=1)
    picked = jnp.sum(
        jnp.where((rank[None, :] == positions[:, None]) & mine[None, :], positions[None, :], 0),
        axis=1,
    ).astype(jnp.int32)
    count = jnp.sum(mine.astype(jnp.int32)).reshape(1)
    first = ((group + groups - groups // 2) % groups).astype(jnp.int32).reshape(1)
    parent = eliminate_parent(
        count, picked, first, child_map, parent_front, got_parent, first_schur, others
    )
    diag = lax.dynamic_update_index_in_dim(diag, diag_got, 1 - member, 0)
    below = lax.dynamic_update_index_in_dim(below, below_got, 1 - member, 0)
    return (diag, below, parent)


def solution(mesh):
    in_specs = (
        P("leaf", "front", None),
        P("leaf", "front", None),
        P("leaf", "front", None),
        P(),
        P(),
        P(),
        P("leaf", "front", None),
    )
    out_specs = (P("leaf", "front", None), P("leaf", "front", None), P("leaf", "front", None))
    return jax.shard_map(
        on_device, mesh=mesh, in_specs=in_specs, out_specs=out_specs, check_vma=False
    )
```

profile of v0, /device:TPU:9, one launch (start us, length us, event | category | flops | bytes accessed | tf_op | source)
XLA Modules:
  0.0 148.4 jit_solution(4359825484062095884)
XLA Ops:
  0.6 0.0 copy-start
  0.7 0.0 copy-start.1
  0.7 0.0 copy-start.2
  0.7 0.0 copy-start.3
  0.7 2.1 %dynamic-slice_bitcast_fusion = f32[576,1152]{1,0:T(8,128)S(1)} fusion(f32[2,576,1152]{2,1,0:T(8,128)} %own_p.1, s32[]{:T(128)S(6)} %select_n.27), kind=kLoop, calls=%fused_computation.2 | loop fusion | bytes 5308420 | tf_op jit(solution)/shard_map/jit(dynamic_index_in_dim)/squeeze | solution.py:441
  2.8 0.7 collective-permute-start
  3.5 0.0 copy-done.1
  3.5 0.4 collective-permute-start.5
  3.9 0.0 copy-done.2
  3.9 0.3 collective-permute-start.1
  4.2 0.0 copy-done.3
  4.2 0.0 copy-start.9
  4.2 0.0 copy-start.4
  4.2 0.4 collective-permute-start.2
  4.6 5.1 %collective-permute-done.2.got_t = f32[96,192]{1,0:T(8,128)S(1)} collective-permute-done((f32[96,192]{1,0:T(8,128)S(1)}, f32[96,192]{1,0:T(8,128)S(1)}, u32[]{:S(2)}, u32[]{:S(2)}) %collective-permute-start.2) | collective-permute-done | bytes 73760 | tf_op jit(solution)/shard_map/ppermute | solution.py:445
  9.7 0.0 collective-permute-done.1.got_l
  9.7 0.0 collective-permute-done.got_p
  9.7 0.0 copy-start.5
  9.7 1.5 %copy-done.5 = f32[576,1152]{1,0:T(8,128)} copy-done((f32[576,1152]{1,0:T(8,128)}, f32[576,1152]{1,0:T(8,128)S(1)}, u32[]{:S(2)}) %copy-start.5) | copy-done | bytes 2654232
  11.2 53.3 %shard_map.94 = (f32[2,576,1152]{2,1,0:T(8,128)}, f32[576,1152]{1,0:T(8,128)}, f32[2,96,1152]{2,1,0:T(8,128)}, f32[96,1152]{1,0:T(8,128)S(1)}, f32[192,128]{1,0:T(8,128)S(1)}) custom-call(f32[2,576,1152]{2,1,0:T(8,128)} %own_p.1, f32[576,1152]{1,0:T(8,128)} %copy-done.5, f32[2,96,1152]{2,1,0:T(8,128)S(1)} %copy-done.2, ...), custom_call_target="tpu_custom_call" | custom-call | tf_op jit(solution)/shard_map/pallas_call | solution.py:331
  64.5 0.4 collective-permute-start.3
  65.0 0.0 copy-done.9
  65.0 0.1 slice.3
  65.1 0.0 copy-done
  65.1 0.7 gather_fusion
  65.8 0.2 collective-permute-start.4
  66.0 0.6 convert_reduce_fusion.1
  66.6 0.0 slice-start
  66.6 0.1 convert_reduce_fusion
  66.7 0.1 select_reduce_fusion.picked
  66.8 20.7 %shard_map.95 = (f32[192,128]{1,0:T(8,128)S(1)}, f32[16,192,128]{2,1,0:T(8,128)S(1)}) custom-call(f32[192,128]{1,0:T(8,128)S(1)} %get-tuple-element.14.packed), custom_call_target="tpu_custom_call" | custom-call | tf_op jit(solution)/shard_map/pallas_call | solution.py:252
  87.5 0.0 collective-permute-done.5.got
  87.6 0.0 copy-done.4
  87.6 0.0 copy-start.7
  87.6 0.0 slice-start.1
  87.6 56.1 %shard_map.96 = f32[1,576,1152]{2,1,0:T(8,128)} custom-call(s32[1]{0:T(128)} %bitcast.6.count, s32[16]{0:T(128)S(1)} %select_reduce_fusion.picked, s32[1]{0:T(128)} %bitcast.7.first, s32[32,192]{1,0:T(8,128)S(1)} %copy-done.4, f32[1,576,1152]{2,1,0:T(8,128)S(1)} %copy-done.1, f32[576,1152]{1,0:T(8,128)} %collective-permute-done.5.got, ...), custom_call_target="tpu_custom_call" | custom-call | tf_op jit(solution)/shard_map/pallas_call | solution.py:418
  143.7 0.0 collective-permute-done.4
  143.7 0.0 copy-done.7
  143.7 0.0 copy-start.8
  143.7 0.0 collective-permute-done.3
  143.7 0.0 slice-done
  143.8 0.0 slice-done.1
  143.8 2.3 %bitcast_dynamic-update-slice_fusion = f32[2,576,1152]{2,1,0:T(8,128)S(1)} fusion(f32[2,576,1152]{2,1,0:T(8,128)S(1)} %bitcast.17, s32[]{:T(128)S(6)} %select_n.27, f32[576,1152]{1,0:T(8,128)} %collective-permute-done.3), kind=kLoop, calls=%fused_computation.1 | loop fusion | bytes 5308420 | tf_op jit(solution)/shard_map/jit(dynamic_update_index_in_dim)/dynamic_update_slice | solution.py:467
  146.0 0.0 copy-done.8
  146.1 0.0 copy-start.6
  146.1 2.4 %copy-done.6 = f32[2,576,1152]{2,1,0:T(8,128)} copy-done((f32[2,576,1152]{2,1,0:T(8,128)}, f32[2,576,1152]{2,1,0:T(8,128)S(1)}, u32[]{:S(2)}) %copy-start.6) | copy-done | bytes 5308440
  (6 shorter events, 0.1 us)
Async XLA Ops:
  0.6 64.5 %copy-start = (s32[16]{0:T(128)S(1)}, s32[16]{0:T(128)}, u32[]{:S(2)}) copy-start(s32[16]{0:T(128)} %param.12) | copy-start | bytes 196
  0.7 2.9 %copy-start.1 = (f32[1,576,1152]{2,1,0:T(8,128)S(1)}, f32[1,576,1152]{2,1,0:T(8,128)}, u32[]{:S(2)}) copy-start(f32[1,576,1152]{2,1,0:T(8,128)} %own.1) | copy-start | bytes 7962628
  0.7 3.2 %copy-start.2 = (f32[2,96,1152]{2,1,0:T(8,128)S(1)}, f32[2,96,1152]{2,1,0:T(8,128)}, u32[]{:S(2)}) copy-start(f32[2,96,1152]{2,1,0:T(8,128)} %own_l.1) | copy-start | bytes 2654212
  0.7 3.5 %copy-start.3 = (f32[2,96,192]{2,1,0:T(8,128)S(1)}, f32[2,96,192]{2,1,0:T(8,128)}, u32[]{:S(2)}) copy-start(f32[2,96,192]{2,1,0:T(8,128)} %own_t.1) | copy-start | bytes 442372
  2.8 6.9 %collective-permute-start = (f32[576,1152]{1,0:T(8,128)S(1)}, f32[576,1152]{1,0:T(8,128)S(1)}, u32[]{:S(2)}, u32[]{:S(2)}) collective-permute-start(f32[576,1152]{1,0:T(8,128)S(1)} %dynamic-slice_bitcast_fusion), channel_id=1, source_target_pairs={{0,1},{1,0},{2,3},{3,2},{4,5},{5,4},{6,7},{7,6},{8,9},{9,8},{10,11... | collective-permute-start | bytes 7962632 | tf_op jit(solution)/shard_map/ppermute | solution.py:443
  3.5 84.0 %collective-permute-start.5 = (f32[576,1152]{1,0:T(8,128)S(1)}, f32[576,1152]{1,0:T(8,128)}, u32[]{:S(2)}, u32[]{:S(2)}) collective-permute-start(f32[576,1152]{1,0:T(8,128)S(1)} %bitcast.15), channel_id=1, source_target_pairs={{0,1},{1,0},{2,3},{3,2},{4,5},{5,4},{6,7},{7,6},{8,9},{9,8},{10,11... | collective-permute-start | bytes 7962632 | tf_op jit(solution)/shard_map/ppermute | solution.py:446
  3.9 5.8 %collective-permute-start.1 = (f32[96,1152]{1,0:T(8,128)S(1)}, f32[96,1152]{1,0:T(8,128)S(1)}, u32[]{:S(2)}, u32[]{:S(2)}) collective-permute-start(f32[96,1152]{1,0:T(8,128)S(1)} %dynamic-slice_bitcast_fusion.1), channel_id=1, source_target_pairs={{0,1},{1,0},{2,3},{3,2},{4,5},{5,4},{6,7},{7,6},{8,9},{9,8},{10,11... | collective-permute-start | bytes 1327112 | tf_op jit(solution)/shard_map/ppermute | solution.py:444
  4.2 60.8 %copy-start.9 = (s32[32,1]{0,1:T(1,128)S(1)}, s32[32,1]{0,1:T(1,128)}, u32[]{:S(2)}) copy-start(s32[32,1]{0,1:T(1,128)} %param.11) | copy-start | bytes 388
  4.2 83.3 %copy-start.4 = (s32[32,192]{1,0:T(8,128)S(1)}, s32[32,192]{1,0:T(8,128)}, u32[]{:S(2)}) copy-start(s32[32,192]{1,0:T(8,128)} %maps.1) | copy-start | bytes 73732
  4.2 5.5 %collective-permute-start.2 = (f32[96,192]{1,0:T(8,128)S(1)}, f32[96,192]{1,0:T(8,128)S(1)}, u32[]{:S(2)}, u32[]{:S(2)}) collective-permute-start(f32[96,192]{1,0:T(8,128)S(1)} %dynamic-slice_bitcast_fusion.2), channel_id=1, source_target_pairs={{0,1},{1,0},{2,3},{3,2},{4,5},{5,4},{6,7},{7,6},{8,9},{9,8},{10,11... | collective-permute-start | bytes 221192 | tf_op jit(solution)/shard_map/ppermute | solution.py:445
  9.7 1.5 %copy-start.5 = (f32[576,1152]{1,0:T(8,128)}, f32[576,1152]{1,0:T(8,128)S(1)}, u32[]{:S(2)}) copy-start(f32[576,1152]{1,0:T(8,128)S(1)} %collective-permute-done.got_p) | copy-start | bytes 7962628
  64.5 79.2 %collective-permute-start.3 = (f32[576,1152]{1,0:T(8,128)}, f32[576,1152]{1,0:T(8,128)}, u32[]{:S(2)}, u32[]{:S(2)}) collective-permute-start(f32[576,1152]{1,0:T(8,128)} %get-tuple-element.11), channel_id=1, source_target_pairs={{0,1},{1,0},{2,3},{3,2},{4,5},{5,4},{6,7},{7,6},{8,9},{9,8},{10,11... | collective-permute-start | bytes 7962632 | tf_op jit(solution)/shard_map/ppermute | solution.py:451
  65.8 77.9 %collective-permute-start.4 = (f32[96,1152]{1,0:T(8,128)S(1)}, f32[96,1152]{1,0:T(8,128)S(1)}, u32[]{:S(2)}, u32[]{:S(2)}) collective-permute-start(f32[96,1152]{1,0:T(8,128)S(1)} %get-tuple-element.13), channel_id=1, source_target_pairs={{0,1},{1,0},{2,3},{3,2},{4,5},{5,4},{6,7},{7,6},{8,9},{9,8},{10,11... | collective-permute-start | bytes 1327112 | tf_op jit(solution)/shard_map/ppermute | solution.py:452
  66.6 77.2 %slice-start = ((s8[5308416]{0:T(1024)(128)(4,1)}), s8[4194304]{0:T(1024)(128)(4,1)S(1)}, s32[]{:S(2)}) async-start(s8[5308416]{0:T(1024)(128)(4,1)} %bitcast.16), calls=%async_computation | async-start | bytes 8388608
  87.6 56.1 %copy-start.7 = (f32[2,96,1152]{2,1,0:T(8,128)S(1)}, f32[2,96,1152]{2,1,0:T(8,128)}, u32[]{:S(2)}) copy-start(f32[2,96,1152]{2,1,0:T(8,128)} %get-tuple-element.12) | copy-start | bytes 2654212
  87.6 56.2 %slice-start.1 = ((s8[5308416]{0:T(1024)(128)(4,1)}), s8[1114112]{0:T(1024)(128)(4,1)S(1)}, s32[]{:S(2)}) async-start(s8[5308416]{0:T(1024)(128)(4,1)} %bitcast.16), calls=%async_computation.1 | async-start | bytes 2228224
  143.7 2.3 %copy-start.8 = (f32[2,96,1152]{2,1,0:T(8,128)}, f32[2,96,1152]{2,1,0:T(8,128)S(1)}, u32[]{:S(2)}) copy-start(f32[2,96,1152]{2,1,0:T(8,128)S(1)} %bitcast_dynamic-update-slice_fusion.1) | copy-start | bytes 2654212
  146.1 2.4 %copy-start.6 = (f32[2,576,1152]{2,1,0:T(8,128)}, f32[2,576,1152]{2,1,0:T(8,128)S(1)}, u32[]{:S(2)}) copy-start(f32[2,576,1152]{2,1,0:T(8,128)S(1)} %bitcast_dynamic-update-slice_fusion) | copy-start | bytes 15925252
where the time goes:
time: 149 us; the launch traced here: 148 us
  Pallas kernels  130 us (87%)
  local copies, waits for them, and re-layouts  9.12 us (6%)
  waiting for transfers between devices  5.11 us (3%)
  starting transfers between devices  2.39 us (2%)
    pallas_call x1, Pallas kernels, eliminate_parent(): pl.pallas_call(parent_kernel, out_shape=jax.ShapeDtypeStruct(own.shape, F...  56.1 us
    pallas_call x1, Pallas kernels, eliminate_child(): pl.pallas_call(child_kernel, out_shape=(jax.ShapeDtypeStruct(own_p.shape,...  53.3 us
    pallas_call x1, Pallas kernels, exchange(): pl.pallas_call(functools.partial(exchange_kernel, groups), out_shape=(jax...  20.7 us
    ppermute x1, waiting for transfers between devices, on_device(): got_tail = lax.ppermute(theirs(child_tail), 'front', swap)  5.1 us
    unnamed x24, local copies, waits for them, and re-layouts  3.94 us
  transfers between devices with their start and end apart: 6, of which 1 were waited for; matrix products, arithmetic and copies ran while one was open for 1% of the time, Pallas kernels for 88%

commit v1 on v0

--- a/solution.py
+++ b/solution.py
@@ -351,8 +351,8 @@
 
 
 def parent_kernel(
-    count, picked, first, maps, own, got, first_schur, others, out,
-    front, panel, work, block, sems,
+    count, picked, first, maps, own, got, first_schur, others, diag_in, diag_got, below_in,
+    below_got, out, diag, below, front, panel, work, block, sems, late_sems,
 ):
     member = lax.axis_index("front")
     half, pivots = got.shape
@@ -368,6 +368,12 @@
         copy.start()
     for copy in copies:
         copy.wait()
+    late = [
+        pltpu.make_async_copy(diag_got, diag.at[1 - member], late_sems.at[0]),
+        pltpu.make_async_copy(below_got, below.at[1 - member], late_sems.at[1]),
+    ]
+    for copy in late:
+        copy.start()
     slot = lax.broadcasted_iota(jnp.int32, (pivots, contrib), 0)
     strip = 3 * NB
 
@@ -408,27 +414,39 @@
     copy = pltpu.make_async_copy(front.at[pl.ds(mine, half), pivot_cols], out.at[0], sems.at[0])
     copy.start()
     copy.wait()
-
-
-def eliminate_parent(count, picked, first, maps, own, got, first_schur, others):
+    for copy in late:
+        copy.wait()
+
+
+def eliminate_parent(
+    count, picked, first, maps, own, got, first_schur, others, diag, diag_got, below, below_got
+):
     half, pivots = got.shape
     anywhere = pl.BlockSpec(memory_space=pl.ANY)
     scalars = pl.BlockSpec(memory_space=pltpu.SMEM)
     vmem = pl.BlockSpec(memory_space=pltpu.VMEM)
     return pl.pallas_call(
         parent_kernel,
-        out_shape=jax.ShapeDtypeStruct(own.shape, F32),
-        in_specs=[scalars] * 3 + [vmem, anywhere, anywhere, vmem, anywhere],
-        out_specs=anywhere,
+        out_shape=(
+            jax.ShapeDtypeStruct(own.shape, F32),
+            jax.ShapeDtypeStruct(diag.shape, F32),
+            jax.ShapeDtypeStruct(below.shape, F32),
+        ),
+        in_specs=[scalars] * 3 + [vmem, anywhere, anywhere, vmem] + [anywhere] * 5,
+        out_specs=(anywhere,) * 3,
+        input_output_aliases={8: 1, 10: 2},
         scratch_shapes=[
             pltpu.VMEM((pivots, padded(pivots)), F32),
             pltpu.VMEM((padded(pivots), 2 * NB), BF16),
             pltpu.VMEM((NB, 2 * NB), F32),
             pltpu.VMEM(first_schur.shape, F32),
             pltpu.SemaphoreType.DMA((2,)),
+            pltpu.SemaphoreType.DMA((2,)),
         ],
         compiler_params=pltpu.CompilerParams(vmem_limit_bytes=48 * 2**20),
-    )(count, picked, first, maps, own, got, first_schur, others)
+    )(
+        count, picked, first, maps, own, got, first_schur, others, diag, diag_got, below, below_got
+    )
 
 
 def on_device(child_pivot, child_lower, child_tail, child_map, child_parent, owner, parent_front):
@@ -461,11 +479,10 @@
     ).astype(jnp.int32)
     count = jnp.sum(mine.astype(jnp.int32)).reshape(1)
     first = ((group + groups - groups // 2) % groups).astype(jnp.int32).reshape(1)
-    parent = eliminate_parent(
-        count, picked, first, child_map, parent_front, got_parent, first_schur, others
-    )
-    diag = lax.dynamic_update_index_in_dim(diag, diag_got, 1 - member, 0)
-    below = lax.dynamic_update_index_in_dim(below, below_got, 1 - member, 0)
+    parent, diag, below = eliminate_parent(
+        count, picked, first, child_map, parent_front, got_parent, first_schur, others,
+        diag, diag_got, below, below_got,
+    )
     return (diag, below, parent)
 
 

time: 149 us -> 173 us (1.16)
  Pallas kernels: 130 us -> 159 us
  local copies, waits for them, and re-layouts: 9.12 us -> 4.41 us
    pallas_call x1, Pallas kernels: 56.1 us -> 84.7 us  [eliminate_parent(): pl.pallas_call(parent_kernel, out_shape=(jax.ShapeDtypeStruct(own.shape,...]
    unnamed x24 -> x14, local copies, waits for them, and re-layouts: 3.94 us -> 1.53 us
    dynamic_update_slice x2 -> x0, local copies, waits for them, and re-layouts: 2.31 us -> none  [the longest x1 2.27 us: on_device(): diag = lax.dynamic_update_index_in_dim(diag, diag_got, 1 - member, 0)]
  transfers between devices with their start and end apart: 6 -> 6, of which waited for: 1 -> 1; matrix products, arithmetic and copies ran while one was open for 1% -> 1% of each run, Pallas kernels for 88% -> 43%
where the time goes in v1:
time: 173 us; the launch traced here: 172 us
  Pallas kernels  159 us (92%)
  waiting for transfers between devices  5.34 us (3%)
  local copies, waits for them, and re-layouts  4.41 us (3%)
  starting transfers between devices  2.12 us (1%)
    pallas_call x1, Pallas kernels, eliminate_parent(): pl.pallas_call(parent_kernel, out_shape=(jax.ShapeDtypeStruct(own.shape,...  84.7 us
    pallas_call x1, Pallas kernels, eliminate_child(): pl.pallas_call(child_kernel, out_shape=(jax.ShapeDtypeStruct(own_p.shape,...  53.3 us
    pallas_call x1, Pallas kernels, exchange(): pl.pallas_call(functools.partial(exchange_kernel, groups), out_shape=(jax...  20.7 us
    ppermute x1, waiting for transfers between devices, on_device(): got_tail = lax.ppermute(theirs(child_tail), 'front', swap)  5.33 us
  transfers between devices with their start and end apart: 6, of which 1 were waited for; matrix products, arithmetic and copies ran while one was open for 1% of the time, Pallas kernels for 43%

profile of v1, /device:TPU:9, one launch (start us, length us, event | category | flops | bytes accessed | tf_op | source)
XLA Modules:
  0.0 172.4 jit_solution(4021210718096934669)
XLA Ops:
  0.6 0.0 copy-start
  0.7 0.0 copy-start.2
  0.7 0.0 copy-start.3
  0.7 0.0 copy-start.1
  0.7 2.1 %dynamic-slice_bitcast_fusion = f32[576,1152]{1,0:T(8,128)S(1)} fusion(f32[2,576,1152]{2,1,0:T(8,128)} %own_p.1, s32[]{:T(128)S(6)} %select_n.26), kind=kLoop, calls=%fused_computation.1 | loop fusion | bytes 5308420 | tf_op jit(solution)/shard_map/jit(dynamic_index_in_dim)/squeeze | solution.py:459
  2.8 0.7 collective-permute-start.1
  3.5 0.0 copy-done.2
  3.5 0.1 collective-permute-start.2
  3.6 0.0 copy-done.3
  3.7 0.5 collective-permute-start.3
  4.2 0.0 copy-done.1
  4.2 0.0 copy-start.6
  4.2 0.0 copy-start.4
  4.2 0.1 collective-permute-start
  4.3 5.3 %collective-permute-done.3.got_t = f32[96,192]{1,0:T(8,128)S(1)} collective-permute-done((f32[96,192]{1,0:T(8,128)S(1)}, f32[96,192]{1,0:T(8,128)S(1)}, u32[]{:S(2)}, u32[]{:S(2)}) %collective-permute-start.3) | collective-permute-done | bytes 73760 | tf_op jit(solution)/shard_map/ppermute | solution.py:463
  9.6 0.0 collective-permute-done.2.got_l
  9.6 0.0 collective-permute-done.1.got_p
  9.6 0.0 copy-start.5
  9.6 1.5 copy-done.5
  11.1 53.3 %shard_map.94 = (f32[2,576,1152]{2,1,0:T(8,128)}, f32[576,1152]{1,0:T(8,128)}, f32[2,96,1152]{2,1,0:T(8,128)}, f32[96,1152]{1,0:T(8,128)S(1)}, f32[192,128]{1,0:T(8,128)S(1)}) custom-call(f32[2,576,1152]{2,1,0:T(8,128)} %own_p.1, f32[576,1152]{1,0:T(8,128)} %copy-done.5, f32[2,96,1152]{2,1,0:T(8,128)S(1)} %copy-done.2, ...), custom_call_target="tpu_custom_call" | custom-call | tf_op jit(solution)/shard_map/pallas_call | solution.py:331
  64.5 0.4 collective-permute-start.4
  64.9 0.0 copy-done.6
  64.9 0.1 slice.3
  65.0 0.0 copy-done
  65.1 0.7 gather_fusion
  65.7 0.2 collective-permute-start.5
  65.9 0.7 convert_reduce_fusion.1
  66.6 0.1 convert_reduce_fusion
  66.7 0.1 select_reduce_fusion.picked
  66.8 20.7 %shard_map.95 = (f32[192,128]{1,0:T(8,128)S(1)}, f32[16,192,128]{2,1,0:T(8,128)S(1)}) custom-call(f32[192,128]{1,0:T(8,128)S(1)} %get-tuple-element.13.packed), custom_call_target="tpu_custom_call" | custom-call | tf_op jit(solution)/shard_map/pallas_call | solution.py:252
  87.5 0.0 collective-permute-done.got
  87.5 0.0 collective-permute-done.5.below_got
  87.5 0.0 collective-permute-done.4.diag_got
  87.5 0.0 copy-done.4
  87.5 84.7 %shard_map.96 = (f32[1,576,1152]{2,1,0:T(8,128)}, f32[2,576,1152]{2,1,0:T(8,128)}, f32[2,96,1152]{2,1,0:T(8,128)}) custom-call(s32[1]{0:T(128)} %bitcast.1.count, s32[16]{0:T(128)S(1)} %select_reduce_fusion.picked, s32[1]{0:T(128)} %bitcast.2.first, s32[32,192]{1,0:T(8,128)S(1)} %copy-done.4, ...), custom_call_target="tpu_custom_call", output_to_operand_aliasing={{1}: (8, {}), {2}: (10, {})} | custom-call | tf_op jit(solution)/shard_map/pallas_call | solution.py:428
  (4 shorter events, 0.0 us)
Async XLA Ops:
  0.6 64.4 %copy-start = (s32[16]{0:T(128)S(1)}, s32[16]{0:T(128)}, u32[]{:S(2)}) copy-start(s32[16]{0:T(128)} %param.12) | copy-start | bytes 196
  0.7 2.9 %copy-start.2 = (f32[2,96,1152]{2,1,0:T(8,128)S(1)}, f32[2,96,1152]{2,1,0:T(8,128)}, u32[]{:S(2)}) copy-start(f32[2,96,1152]{2,1,0:T(8,128)} %own_l.1) | copy-start | bytes 2654212
  0.7 3.0 %copy-start.3 = (f32[2,96,192]{2,1,0:T(8,128)S(1)}, f32[2,96,192]{2,1,0:T(8,128)}, u32[]{:S(2)}) copy-start(f32[2,96,192]{2,1,0:T(8,128)} %own_t.1) | copy-start | bytes 442372
  0.7 3.5 %copy-start.1 = (f32[1,576,1152]{2,1,0:T(8,128)S(1)}, f32[1,576,1152]{2,1,0:T(8,128)}, u32[]{:S(2)}) copy-start(f32[1,576,1152]{2,1,0:T(8,128)} %own.1) | copy-start | bytes 7962628
  2.8 6.9 %collective-permute-start.1 = (f32[576,1152]{1,0:T(8,128)S(1)}, f32[576,1152]{1,0:T(8,128)S(1)}, u32[]{:S(2)}, u32[]{:S(2)}) collective-permute-start(f32[576,1152]{1,0:T(8,128)S(1)} %dynamic-slice_bitcast_fusion), channel_id=1, source_target_pairs={{0,1},{1,0},{2,3},{3,2},{4,5},{5,4},{6,7},{7,6},{8,9},{9,8},{10,11... | collective-permute-start | bytes 7962632 | tf_op jit(solution)/shard_map/ppermute | solution.py:461
  3.5 6.1 %collective-permute-start.2 = (f32[96,1152]{1,0:T(8,128)S(1)}, f32[96,1152]{1,0:T(8,128)S(1)}, u32[]{:S(2)}, u32[]{:S(2)}) collective-permute-start(f32[96,1152]{1,0:T(8,128)S(1)} %dynamic-slice_bitcast_fusion.1), channel_id=1, source_target_pairs={{0,1},{1,0},{2,3},{3,2},{4,5},{5,4},{6,7},{7,6},{8,9},{9,8},{10,11... | collective-permute-start | bytes 1327112 | tf_op jit(solution)/shard_map/ppermute | solution.py:462
  3.7 6.0 %collective-permute-start.3 = (f32[96,192]{1,0:T(8,128)S(1)}, f32[96,192]{1,0:T(8,128)S(1)}, u32[]{:S(2)}, u32[]{:S(2)}) collective-permute-start(f32[96,192]{1,0:T(8,128)S(1)} %dynamic-slice_bitcast_fusion.2), channel_id=1, source_target_pairs={{0,1},{1,0},{2,3},{3,2},{4,5},{5,4},{6,7},{7,6},{8,9},{9,8},{10,11... | collective-permute-start | bytes 221192 | tf_op jit(solution)/shard_map/ppermute | solution.py:463
  4.2 60.7 %copy-start.6 = (s32[32,1]{0,1:T(1,128)S(1)}, s32[32,1]{0,1:T(1,128)}, u32[]{:S(2)}) copy-start(s32[32,1]{0,1:T(1,128)} %param.11) | copy-start | bytes 388
  4.2 83.3 %copy-start.4 = (s32[32,192]{1,0:T(8,128)S(1)}, s32[32,192]{1,0:T(8,128)}, u32[]{:S(2)}) copy-start(s32[32,192]{1,0:T(8,128)} %maps.1) | copy-start | bytes 73732
  4.2 83.3 %collective-permute-start = (f32[576,1152]{1,0:T(8,128)S(1)}, f32[576,1152]{1,0:T(8,128)}, u32[]{:S(2)}, u32[]{:S(2)}) collective-permute-start(f32[576,1152]{1,0:T(8,128)S(1)} %bitcast.11), channel_id=1, source_target_pairs={{0,1},{1,0},{2,3},{3,2},{4,5},{5,4},{6,7},{7,6},{8,9},{9,8},{10,11... | collective-permute-start | bytes 7962632 | tf_op jit(solution)/shard_map/ppermute | solution.py:464
  9.6 1.5 copy-start.5
  64.5 23.1 %collective-permute-start.4 = (f32[576,1152]{1,0:T(8,128)}, f32[576,1152]{1,0:T(8,128)}, u32[]{:S(2)}, u32[]{:S(2)}) collective-permute-start(f32[576,1152]{1,0:T(8,128)} %get-tuple-element.17), channel_id=1, source_target_pairs={{0,1},{1,0},{2,3},{3,2},{4,5},{5,4},{6,7},{7,6},{8,9},{9,8},{10,11... | collective-permute-start | bytes 7962632 | tf_op jit(solution)/shard_map/ppermute | solution.py:469
  65.7 21.8 %collective-permute-start.5 = (f32[96,1152]{1,0:T(8,128)S(1)}, f32[96,1152]{1,0:T(8,128)S(1)}, u32[]{:S(2)}, u32[]{:S(2)}) collective-permute-start(f32[96,1152]{1,0:T(8,128)S(1)} %get-tuple-element.19), channel_id=1, source_target_pairs={{0,1},{1,0},{2,3},{3,2},{4,5},{5,4},{6,7},{7,6},{8,9},{9,8},{10,11... | collective-permute-start | bytes 1327112 | tf_op jit(solution)/shard_map/ppermute | solution.py:470
